TPU v7x, 32 devices: a whole 2x2x4 slice. The times are simulated.
32 devices in a mesh: seq: 8 (over y, x, core), exp: 4 (over z).
Axes of the slice: x: 2, y: 2, z: 4, core: 2. Of those that a mesh axis runs over, the one named last changes fastest.
Arguments:
- query_proj: bfloat16 [512, 4096], P('seq', 'exp'), may hold values from -6 to 6
- key_proj: bfloat16 [512, 4096], P('seq', 'exp'), may hold values from -6 to 6
- value_proj: bfloat16 [512, 4096], P('seq', 'exp'), may hold values from -6 to 6
- residual: bfloat16 [512, 6144], P(('seq', 'exp')), may hold values from -6 to 6
- out_weight: bfloat16 [6144, 4096], P('seq', 'exp'), may hold values from -0.09375 to 0.09375
- expert_ids: int32 [512, 2], P(('seq', 'exp')), may hold values from 0 to 3, all different within a row; in each aligned block of 16 rows (0 to 15, 16 to 31, ...) at most 12 rows name the same one
- gate_values: float32 [512, 2], P(('seq', 'exp')), may hold values from 0.2 to 1
- w_gate: bfloat16 [4, 9216, 6144], P('exp', 'seq'), may hold values from -0.078125 to 0.078125
- w_up: bfloat16 [4, 9216, 6144], P('exp', 'seq'), may hold values from -0.078125 to 0.078125
- w_down: bfloat16 [4, 9216, 6144], P('exp', 'seq'), may hold values from -0.0625 to 0.0625
Outputs:
- mixed: bfloat16 [512, 6144], P(('seq', 'exp'))
Inputs may be any that keep to these rules, and one draw needn't show every extreme that they name: `expert_ids`: within the 16 rows of one device no expert is named more than 12 times, a bound that some block reaches; the 2 experts of a row differ.
All inputs are finite; a program needn't handle non-finite values.
Results may differ from a plain program's by a relative error of at most 0.018.
Values may be sent and summed in bfloat16 or wider, within the bound.
A program may use at most 128 MiB of HBM per device.

v0:
```python
import jax
import jax.numpy as jnp
from jax import lax
from jax.sharding import PartitionSpec as P

HD = 128
TOP = 2


def entering(array, axis, combine, identity):
    devices, place = (lax.axis_size(axis), lax.axis_index(axis))
    everything = lax.all_gather(array.astype(jnp.bfloat16), axis)
    start = jnp.broadcast_to(jnp.asarray(identity, array.dtype), array.shape)

    def hop(k, before):
        reached = k < place
        new = combine(before, everything[k].astype(array.dtype))
        return jnp.where(reached, new, before)

    return lax.fori_loop(0, devices, hop, start)


def features(x):
    widened = x.astype(jnp.float32)
    return (widened * jax.nn.sigmoid(widened)).astype(jnp.bfloat16)


def times_rows(left, right):
    return lax.dot_general(
        left, right, (((1,), (1,)), ((), ())), preferred_element_type=jnp.float32
    )


def local(
    query_proj,
    key_proj,
    value_proj,
    residual,
    out_weight,
    expert_ids,
    gate_values,
    w_gate,
    w_up,
    w_down,
):
    tokens_here = query_proj.shape[0]
    heads_here = query_proj.shape[1] // HD
    query_feat = features(query_proj).reshape(tokens_here, heads_here, HD)
    key_feat = features(key_proj).reshape(tokens_here, heads_here, HD)
    value_rows = value_proj.reshape(tokens_here, heads_here, HD)
    span_state = jnp.einsum(
        "thd,the->hde", key_feat, value_rows, preferred_element_type=jnp.float32
    )
    earlier = entering(span_state, "seq", lambda a, b: a + b, jnp.zeros_like(span_state))
    prefix = earlier.astype(jnp.bfloat16)
    earlier_term = jnp.einsum(
        "thd,hde->the", query_feat, prefix, preferred_element_type=jnp.float32
    )
    scores = jnp.einsum("thd,shd->hts", query_feat, key_feat, preferred_element_type=jnp.float32)
    causal = jnp.arange(tokens_here)[:, None] >= jnp.arange(tokens_here)[None, :]
    weights = jnp.where(causal[None], scores, 0.0).astype(jnp.bfloat16)
    local_term = jnp.einsum("hts,she->the", weights, value_rows, preferred_element_type=jnp.float32)
    combined = local_term + earlier_term
    normed = combined * lax.rsqrt(jnp.mean(combined * combined, axis=-1, keepdims=True) + 1e-06)
    normed = normed.astype(jnp.bfloat16).reshape(tokens_here, heads_here * HD)
    partial_out = times_rows(normed, lax.all_gather(out_weight, "seq", axis=0, tiled=True))
    summed = lax.psum_scatter(
        partial_out.astype(jnp.bfloat16), "exp", scatter_dimension=0, tiled=True
    ).astype(jnp.float32)
    mixed_in = (residual.astype(jnp.float32) + summed).astype(jnp.bfloat16)
    groups = lax.axis_size("exp")
    tok_sub = residual.shape[0]
    capacity = max(2, (3 * tok_sub * TOP + 2 * groups - 1) // (2 * groups))
    local_rows = groups * capacity
    chosen = expert_ids.reshape(-1)
    onehot = (chosen[:, None] == jnp.arange(groups, dtype=jnp.int32)[None, :]).astype(jnp.int32)
    before = jnp.cumsum(onehot, axis=0) - onehot
    slot_index = jnp.sum(before * onehot, axis=1)
    target = chosen * capacity + slot_index
    targets = target.reshape(tok_sub, TOP)
    slot_ids = jnp.arange(local_rows, dtype=jnp.int32)
    placing = jnp.any(slot_ids[:, None, None] == targets[None, :, :], axis=2).astype(jnp.bfloat16)
    outgoing = jnp.dot(placing, mixed_in, preferred_element_type=jnp.float32).astype(jnp.bfloat16)
    outgoing = outgoing.reshape(groups, capacity, -1)
    gate_local = w_gate[0]
    up_local = w_up[0]
    down_local = w_down[0]
    hidden_here = gate_local.shape[0]
    arrived = lax.all_to_all(outgoing, "exp", split_axis=0, concat_axis=0, tiled=True).reshape(
        local_rows, -1
    )
    rows_part = lax.all_gather(arrived, "seq", axis=0, tiled=True)
    acts = jnp.concatenate(
        [times_rows(rows_part, gate_local), times_rows(rows_part, up_local)], axis=1
    )
    gate_act = acts[:, :hidden_here]
    up_act = acts[:, hidden_here:]
    activated = (jax.nn.silu(gate_act) * up_act).astype(jnp.bfloat16)
    rows_part = activated
    expert_sums = lax.psum_scatter(
        jnp.dot(rows_part, down_local, preferred_element_type=jnp.float32).astype(jnp.bfloat16),
        "seq",
        scatter_dimension=0,
        tiled=True,
    )
    expert_out = expert_sums.reshape(groups, capacity, -1)
    returned = lax.all_to_all(expert_out, "exp", split_axis=0, concat_axis=0, tiled=True).reshape(
        local_rows, -1
    )
    picked = returned[target].astype(jnp.float32).reshape(tok_sub, TOP, -1)
    mixed = mixed_in.astype(jnp.float32) + jnp.sum(gate_values[:, :, None] * picked, axis=1)
    return mixed.astype(jnp.bfloat16)


def solution(mesh):
    return jax.shard_map(
        local,
        mesh=mesh,
        in_specs=(
            P("seq", "exp"),
            P("seq", "exp"),
            P("seq", "exp"),
            P(("seq", "exp"), None),
            P("seq", "exp"),
            P(("seq", "exp"), None),
            P(("seq", "exp"), None),
            P("exp", "seq", None),
            P("exp", "seq", None),
            P("exp", "seq", None),
        ),
        out_specs=P(("seq", "exp"), None),
        check_vma=False,
    )
```

profile of v0, /device:TPU:9, one launch (start us, length us, event | category | flops | bytes accessed | tf_op | source)
XLA Modules:
  0.0 329.2 jit_solution(14853857434425266002)
XLA Ops:
  6.5 1.1 fusion.35
  9.9 28.9 %all-gather.9.cloned.1.call-done = bf16[64,128,128]{2,1,0:T(8,128)(2,1)} async-done(((bf16[8,128,128]{2,1,0:T(8,128)(2,1)}), bf16[64,128,128]{2,1,0:T(8,128)(2,1)}) %all-gather.9.cloned.1.call-update) | async-done | bytes 2097168 | tf_op jit(solution)/shard_map/all_gather | solution.py:12
  38.8 10.1 %while.14 = (s32[]{:T(128)}, f32[8,128,128]{2,1,0:T(8,128)S(1)}, s32[]{:T(128)}, bf16[8,8,128,128]{3,2,1,0:T(8,128)(2,1)}, s32[]{:T(128)}, /*index=5*/s32[]{:T(128)}) while((s32[]{:T(128)}, f32[8,128,128]{2,1,0:T(8,128)S(1)}, s32[]{:T(128)}, bf16[8,8,128,128]{3,2,1,0:T(8,128)(2,1)}, s32[]{:T(128)}, /*index=5*/s32[]{:T(128)}) %tuple.48), condition=%wide.region_1.2_spmd.clone, body=%wide.region_0.1_spmd.clone.sunk | while | flops 524292 | bytes 1310813 | solution.py:20
  38.8 1.2 add_select_fusion.2
  40.0 1.2 add_select_fusion.2
  41.3 1.2 add_select_fusion.2
  42.5 1.2 add_select_fusion.2
  43.8 1.2 add_select_fusion.2
  45.1 1.2 add_select_fusion.2
  46.3 1.2 add_select_fusion.2
  47.6 1.3 add_select_fusion.2
  49.2 63.6 %all-gather.5.cloned.1.call-done = bf16[6144,1024]{1,0:T(8,128)(2,1)} async-done(((bf16[768,1024]{1,0:T(8,128)(2,1)}), bf16[6144,1024]{1,0:T(8,128)(2,1)}) %all-gather.5.cloned.1.call-update) | async-done | bytes 12582928 | tf_op jit(solution)/shard_map/all_gather | solution.py:66
  112.8 9.5 %convolution_convert_fusion = bf16[64,6144]{1,0:T(8,128)(2,1)} fusion(bf16[6144,1024]{1,0:T(8,128)(2,1)} %all-gather.5.cloned.1.call-done, f32[64,8,128]{2,0,1:T(8,128)S(1)} %get-tuple-element.111, f32[64,8]{0,1:T(8,128)S(1)} %add_rsqrt_fusion), kind=kOutput, calls=%fused_computation.9 | convolution fusion | flops 805830656 | bytes 13633536 | tf_op jit(solution)/shard_map/dot_general | solution.py:29
  123.8 19.4 %reduce-scatter.3.cloned.1.call-done = bf16[16,6144]{1,0:T(8,128)(2,1)} async-done(((bf16[64,6144]{1,0:T(8,128)(2,1)}), bf16[16,6144]{1,0:T(8,128)(2,1)}) %reduce-scatter.3.cloned.1.call-update) | async-done | bytes 196624 | tf_op jit(solution)/shard_map/reduce_scatter | solution.py:67
  143.2 1.3 convolution_convert_fusion.1
  144.6 21.9 %all_to_all.10 = bf16[4,12,6144]{2,1,0:T(8,128)(2,1)S(1)} all-to-all(bf16[4,12,6144]{2,1,0:T(8,128)(2,1)S(1)} %reshape.91), channel_id=1, replica_groups=mesh['seq'=8,'exp'=4] {'exp'}, dimensions={0} | all-to-all | bytes 1179648 | tf_op jit(solution)/shard_map/all_to_all | solution.py:89
  167.8 41.2 %all-gather.7.cloned.1.call-done = bf16[384,6144]{1,0:T(8,128)(2,1)} async-done(((bf16[48,6144]{1,0:T(8,128)(2,1)}), bf16[384,6144]{1,0:T(8,128)(2,1)}) %all-gather.7.cloned.1.call-update) | async-done | bytes 4718608 | tf_op jit(solution)/shard_map/all_gather | solution.py:92
  209.0 10.2 %fusion.4 = f32[384,1152]{1,0:T(8,128)S(1)} fusion(bf16[384,6144]{1,0:T(8,128)(2,1)} %all-gather.7.cloned.1.call-done, bf16[1,1152,6144]{2,1,0:T(8,128)(2,1)} %param.19), kind=kOutput, calls=%fused_computation.6 | convolution fusion | flops 5435817984 | bytes 20643840 | tf_op jit(solution)/shard_map/dot_general | solution.py:29
  219.2 23.4 %fusion.6 = bf16[384,6144]{1,0:T(8,128)(2,1)} fusion(bf16[1,1152,6144]{2,1,0:T(8,128)(2,1)} %param.21, bf16[384,6144]{1,0:T(8,128)(2,1)} %all-gather.7.cloned.1.call-done, bf16[1,1152,6144]{2,1,0:T(8,128)(2,1)} %param.20, f32[384,1152]{1,0:T(8,128)S(1)} %fusion.4), kind=kOutput, calls=%fused_computation.8 | convolution fusion | flops 10876649472 | bytes 39518208 | tf_op jit(solution)/shard_map/dot_general | solution.py:101
  242.7 53.6 %reduce-scatter.5.cloned.1.call-done = bf16[48,6144]{1,0:T(8,128)(2,1)} async-done(((bf16[384,6144]{1,0:T(8,128)(2,1)}), bf16[48,6144]{1,0:T(8,128)(2,1)}) %reduce-scatter.5.cloned.1.call-update) | async-done | bytes 589840 | tf_op jit(solution)/shard_map/reduce_scatter | solution.py:100
  296.3 2.1 reshape.93
  298.4 4.7 %all-to-all-start.1 = ((bf16[4,12,6144]{2,1,0:T(8,128)(2,1)}), bf16[4,12,6144]{2,1,0:T(8,128)(2,1)S(1)}, u32[]{:S(2)}, u32[]{:S(2)}) async-start(bf16[4,12,6144]{2,1,0:T(8,128)(2,1)} %reshape.93), calls=%async_computation.3 | async-start | bytes 1572864 | tf_op jit(solution)/shard_map/all_to_all | solution.py:107
  303.4 16.0 %all-to-all-done.1 = bf16[4,12,6144]{2,1,0:T(8,128)(2,1)S(1)} async-done(((bf16[4,12,6144]{2,1,0:T(8,128)(2,1)}), bf16[4,12,6144]{2,1,0:T(8,128)(2,1)S(1)}, u32[]{:S(2)}, u32[]{:S(2)}) %all-to-all-start.1) | async-done | bytes 589856 | tf_op jit(solution)/shard_map/all_to_all | solution.py:107
  320.8 1.1 multiply_reduce_fusion
  (55 shorter events, 7.6 us)
Async XLA Ops:
  6.5 1.2 copy-start
  6.5 32.2 %all-gather.9.cloned.1.call-start = ((), (), s32[]{:S(2)}) async-start(), calls=%async_computation.8 | async-start | bytes 2359296 | tf_op jit(solution)/shard_map/all_gather | solution.py:12
  8.7 104.1 %all-gather.5.cloned.1.call-start = ((), (), s32[]{:S(2)}) async-start(), calls=%async_computation.4 | async-start | bytes 14155776 | tf_op jit(solution)/shard_map/all_gather | solution.py:66
  9.5 133.7 %reduce-scatter.3.cloned.1.call-start = ((), (), s32[]{:S(2)}) async-start(), calls=%async_computation.5 | async-start | bytes 983040 | tf_op jit(solution)/shard_map/reduce_scatter | solution.py:67
  112.8 9.6 %copy-start.8 = (s32[16,2]{0,1:T(2,128)S(1)}, s32[16,2]{0,1:T(2,128)}, u32[]{:S(2)}) copy-start(s32[16,2]{0,1:T(2,128)} %param.17) | copy-start | bytes 388
  112.8 30.4 %copy-start.2 = (bf16[16,6144]{1,0:T(8,128)(2,1)S(1)}, bf16[16,6144]{1,0:T(8,128)(2,1)}, u32[]{:S(2)}) copy-start(bf16[16,6144]{1,0:T(8,128)(2,1)} %param.15) | copy-start | bytes 589828
  122.4 86.6 %all-gather.7.cloned.1.call-start = ((), (), s32[]{:S(2)}) async-start(), calls=%async_computation.6 | async-start | bytes 5308416 | tf_op jit(solution)/shard_map/all_gather | solution.py:92
  122.9 96.3 %copy-start.6 = (s32[32]{0:T(128)}, s32[32]{0:T(128)S(1)}, u32[]{:S(2)}) copy-start(s32[32]{0:T(128)S(1)} %select_reduce_fusion) | copy-start | bytes 388
  167.5 128.8 %reduce-scatter.5.cloned.1.call-start = ((), (), s32[]{:S(2)}) async-start(), calls=%async_computation.7 | async-start | bytes 5308416 | tf_op jit(solution)/shard_map/reduce_scatter | solution.py:100
  242.6 60.5 %copy-start.5 = (s32[16,2]{1,0:T(8,128)S(1)}, s32[16,2]{1,0:T(8,128)}, u32[]{:S(2)}) copy-start(s32[16,2]{1,0:T(8,128)} %get-tuple-element.108) | copy-start | bytes 388
  242.6 60.6 %copy-start.9 = (f32[16,2]{0,1:T(2,128)S(1)}, f32[16,2]{0,1:T(2,128)}, u32[]{:S(2)}) copy-start(f32[16,2]{0,1:T(2,128)} %param.18) | copy-start | bytes 388
  242.7 60.7 %copy-start.7 = (s32[32]{0:T(128)S(1)}, s32[32]{0:T(128)}, u32[]{:S(2)}) copy-start(s32[32]{0:T(128)} %copy-done.6) | copy-start | bytes 388
  296.3 26.3 %copy-start.1 = (bf16[64,1024]{1,0:T(8,128)(2,1)S(1)}, bf16[64,1024]{1,0:T(8,128)(2,1)}, u32[]{:S(2)}) copy-start(bf16[64,1024]{1,0:T(8,128)(2,1)} %param.14) | copy-start | bytes 393220
  298.4 23.4 %copy-start.3 = (bf16[16,6144]{1,0:T(8,128)(2,1)S(1)}, bf16[16,6144]{1,0:T(8,128)(2,1)}, u32[]{:S(2)}) copy-start(bf16[16,6144]{1,0:T(8,128)(2,1)} %param.15) | copy-start | bytes 589828
  298.4 23.5 %copy-start.4 = (bf16[16,6144]{1,0:T(8,128)(2,1)S(1)}, bf16[16,6144]{1,0:T(8,128)(2,1)}, u32[]{:S(2)}) copy-start(bf16[16,6144]{1,0:T(8,128)(2,1)} %reduce-scatter.3.cloned.1.call-done) | copy-start | bytes 589828
  298.4 20.9 %all-to-all-start.1 = ((bf16[4,12,6144]{2,1,0:T(8,128)(2,1)}), bf16[4,12,6144]{2,1,0:T(8,128)(2,1)S(1)}, u32[]{:S(2)}, u32[]{:S(2)}) async-start(bf16[4,12,6144]{2,1,0:T(8,128)(2,1)} %reshape.93), calls=%async_computation.3 | async-start | bytes 1572864 | tf_op jit(solution)/shard_map/all_to_all | solution.py:107
Sparse Core Ops, SparseCore 0:
  9.2 29.4 all-gather.8
  40.7 72.1 all-gather.4
  122.5 20.6 reduce-scatter.2
  167.6 41.2 all-gather.6
  242.8 53.4 reduce-scatter.4
where the time goes:
time: 335 us; the launch traced here: 329 us
  waiting for transfers between devices  224 us (67%)
  matrix products  46.1 us (14%)
  blocking collectives  21.9 us (7%)
  other arithmetic  13.9 us (4%)
  between operations  13.3 us (4%)
  local copies, waits for them, and re-layouts  5.19 us (2%)
  starting transfers between devices  5.06 us (2%)
    all_gather x1, waiting for transfers between devices, local(): lax.all_gather(out_weight, 'seq', axis=0, tiled=True)  63.6 us
    reduce_scatter x1, waiting for transfers between devices, local(): lax.psum_scatter(jnp.dot(rows_part, down_local, preferred_element_type=jn...  53.6 us
    all_gather x1, waiting for transfers between devices, local(): rows_part = lax.all_gather(arrived, 'seq', axis=0, tiled=True)  41.2 us
    all_gather x1, waiting for transfers between devices, entering(): everything = lax.all_gather(array.astype(jnp.bfloat16), axis)  28.9 us
    dot_general x1, matrix products, local(): jnp.dot(rows_part, down_local, preferred_element_type=jnp.float32)  23.4 us
    all_to_all x1, blocking collectives, local(): lax.all_to_all(outgoing, 'exp', split_axis=0, concat_axis=0, tiled=True)  21.9 us
    dot_general x2, matrix products, times_rows(): lax.dot_general(left, right, (((1,), (1,)), ((), ())), preferred_element_...  19.8 us
    reduce_scatter x1, waiting for transfers between devices, local(): lax.psum_scatter(partial_out.astype(jnp.bfloat16), 'exp', scatter_dimensi...  19.4 us
  transfers between devices with their start and end apart: 6, of which 6 were waited for; matrix products, arithmetic and copies ran while one was open for 4% of the time, Pallas kernels for 0%

commit v1 on v0

--- a/solution.py
+++ b/solution.py
@@ -1,6 +1,10 @@
+import functools
+
 import jax
 import jax.numpy as jnp
 from jax import lax
+from jax.experimental import pallas as pl
+from jax.experimental.pallas import tpu as pltpu
 from jax.sharding import PartitionSpec as P
 
 HD = 128
@@ -74,7 +78,8 @@
     local_rows = groups * capacity
     chosen = expert_ids.reshape(-1)
     onehot = (chosen[:, None] == jnp.arange(groups, dtype=jnp.int32)[None, :]).astype(jnp.int32)
-    before = jnp.cumsum(onehot, axis=0) - onehot
+    place = jnp.arange(tok_sub * TOP)
+    before = jnp.sum((place[:, None] > place[None, :])[:, :, None] * onehot[None], axis=1)
     slot_index = jnp.sum(before * onehot, axis=1)
     target = chosen * capacity + slot_index
     targets = target.reshape(tok_sub, TOP)
@@ -112,9 +117,338 @@
     return mixed.astype(jnp.bfloat16)
 
 
+MESH = pl.DeviceIdType.MESH
+VMEM = pltpu.VMEM
+
+
+def _place(ref, kind, size, i):
+    if kind == "row":
+        return ref.at[pl.ds(pl.multiple_of(i * size, size), size), :]
+    if kind == "col":
+        return ref.at[:, pl.ds(pl.multiple_of(i * size, size), size)]
+    return ref
+
+
+def _greet(axis, peers):
+    barrier = pltpu.get_barrier_semaphore()
+    for peer in peers:
+        pl.semaphore_signal(barrier, inc=1, device_id={axis: peer}, device_id_type=MESH)
+    pl.semaphore_wait(barrier, len(peers))
+
+
+def _exchange_kernel(axis, n, kinds, *refs):
+    m = len(kinds)
+    ins, outs = refs[:m], refs[m : 2 * m]
+    send, recv, own = refs[2 * m :]
+    me = lax.axis_index(axis)
+    peers = [lax.rem(me + k, n) for k in range(1, n)]
+    _greet(axis, peers)
+    copies = []
+    for k, peer in enumerate(peers):
+        for a, (sk, ss, dk, ds) in enumerate(kinds):
+            c = pltpu.make_async_remote_copy(
+                src_ref=_place(ins[a], sk, ss, peer),
+                dst_ref=_place(outs[a], dk, ds, me),
+                send_sem=send.at[a, k],
+                recv_sem=recv.at[a, k],
+                device_id={axis: peer},
+                device_id_type=MESH,
+            )
+            c.start()
+            copies.append(c)
+    for a, (sk, ss, dk, ds) in enumerate(kinds):
+        c = pltpu.make_async_copy(
+            _place(ins[a], sk, ss, me), _place(outs[a], dk, ds, me), own.at[a]
+        )
+        c.start()
+        copies.append(c)
+    for c in copies:
+        c.wait()
+
+
+def exchange(axis, kinds, ins, out_shapes, cid):
+    n, m = lax.axis_size(axis), len(ins)
+    return pl.pallas_call(
+        functools.partial(_exchange_kernel, axis, n, kinds),
+        out_shape=out_shapes,
+        in_specs=[pl.BlockSpec(memory_space=VMEM)] * m,
+        out_specs=[pl.BlockSpec(memory_space=VMEM)] * m,
+        scratch_shapes=[
+            pltpu.SemaphoreType.DMA((m, n - 1)),
+            pltpu.SemaphoreType.DMA((m, n - 1)),
+            pltpu.SemaphoreType.DMA((m,)),
+        ],
+        compiler_params=pltpu.CompilerParams(
+            collective_id=cid, has_side_effects=True, vmem_limit_bytes=32 << 20
+        ),
+    )(*ins)
+
+
+def _around(s):
+    c, x, y = lax.rem(s, 2), lax.rem(s // 2, 2), s // 4
+    right = s + 2 - 4 * x
+    up = s + 4 - 8 * y
+    return right, up, up + 2 - 4 * x, 1 - 2 * c
+
+
+def _gather_kernel(rows, width, in_ref, out_ref, send, recv, own):
+    s = lax.axis_index("seq")
+    sx, sy, sd, flip = _around(s)
+    sib = s + flip
+    half = rows // 2
+
+    def at(i, part=None):
+        cols = pl.ds(pl.multiple_of(i * width, width), width)
+        if part is None:
+            return out_ref.at[:, cols]
+        return out_ref.at[pl.ds(part * half, half), cols]
+
+    def push(src, dst, to, k):
+        c = pltpu.make_async_remote_copy(
+            src_ref=src, dst_ref=dst, send_sem=send.at[k], recv_sem=recv.at[k],
+            device_id={"seq": to}, device_id_type=MESH,
+        )
+        c.start()
+        return c
+
+    _greet("seq", [sx, sy, sib])
+    to_x = push(in_ref, at(s), sx, 0)
+    to_y = push(in_ref, at(s), sy, 1)
+    to_s = push(in_ref, at(s), sib, 2)
+    mine = pltpu.make_async_copy(in_ref, at(s), own)
+    mine.start()
+    to_x.wait_recv()
+    fy = push(at(sx, 0), at(sx, 0), sy, 3)
+    gx = push(at(sx), at(sx), sib, 4)
+    to_y.wait_recv()
+    fx = push(at(sy, 1), at(sy, 1), sx, 5)
+    gy = push(at(sy), at(sy), sib, 6)
+    fy.wait_recv()
+    fx.wait_recv()
+    gd = push(at(sd), at(sd), sib, 7)
+    to_s.wait_recv()
+    gx.wait_recv()
+    gy.wait_recv()
+    gd.wait_recv()
+    for c in (to_x, to_y, to_s, fy, gx, fx, gy, gd):
+        c.wait_send()
+    mine.wait()
+
+
+def gather_columns(x, cid):
+    rows, width = x.shape
+    n = lax.axis_size("seq")
+    return pl.pallas_call(
+        functools.partial(_gather_kernel, rows, width),
+        out_shape=jax.ShapeDtypeStruct((rows, n * width), x.dtype),
+        in_specs=[pl.BlockSpec(memory_space=VMEM)],
+        out_specs=pl.BlockSpec(memory_space=VMEM),
+        scratch_shapes=[
+            pltpu.SemaphoreType.DMA((8,)),
+            pltpu.SemaphoreType.DMA((8,)),
+            pltpu.SemaphoreType.DMA,
+        ],
+        compiler_params=pltpu.CompilerParams(
+            collective_id=cid, has_side_effects=True, vmem_limit_bytes=32 << 20
+        ),
+    )(x)
+
+
+def _scatter_kernel(rows, width, in_ref, out_ref, rs, st, rd, rx, ry, send, recv):
+    s = lax.axis_index("seq")
+    sx, sy, sd, flip = _around(s)
+    sib = s + flip
+    half = rows // 2
+    step = 32
+
+    def part(i):
+        return in_ref.at[:, pl.ds(pl.multiple_of(i * width, width), width)]
+
+    def push(src, dst, to, k):
+        c = pltpu.make_async_remote_copy(
+            src_ref=src, dst_ref=dst, send_sem=send.at[k], recv_sem=recv.at[k],
+            device_id={"seq": to}, device_id_type=MESH,
+        )
+        c.start()
+        return c
+
+    def add(dst, d0, count, terms):
+        @pl.loop(0, count // step)
+        def _(i):
+            total = None
+            for ref, base in terms:
+                v = ref[pl.ds(pl.multiple_of(base + i * step, step), step), :].astype(jnp.float32)
+                total = v if total is None else total + v
+            dst[pl.ds(pl.multiple_of(d0 + i * step, step), step), :] = total.astype(dst.dtype)
+
+    def top(ref):
+        return ref.at[pl.ds(0, half), :]
+
+    def bottom(ref):
+        return ref.at[pl.ds(half, half), :]
+
+    _greet("seq", [sx, sy, sib])
+    cs = [push(part(i + flip), rs.at[k], sib, k) for k, i in enumerate((sd, sx, sy, s))]
+    cs[0].wait_recv()
+    add(st.at[0], 0, rows, [(part(sd), 0), (rs.at[0], 0)])
+    dt = push(top(st.at[0]), rd.at[0], sx, 4)
+    db = push(bottom(st.at[0]), rd.at[1], sy, 5)
+    cs[1].wait_recv()
+    add(st.at[1], 0, rows, [(part(sx), 0), (rs.at[1], 0)])
+    xt = push(top(st.at[1]), top(rx), sx, 6)
+    cs[2].wait_recv()
+    add(st.at[2], 0, rows, [(part(sy), 0), (rs.at[2], 0)])
+    yb = push(bottom(st.at[2]), bottom(ry), sy, 7)
+    cs[3].wait_recv()
+    dt.wait_recv()
+    add(st.at[2], 0, half, [(st.at[2], 0), (rd.at[0], 0)])
+    yt = push(top(st.at[2]), top(ry), sy, 8)
+    db.wait_recv()
+    add(st.at[1], half, half, [(st.at[1], half), (rd.at[1], 0)])
+    xb = push(bottom(st.at[1]), bottom(rx), sx, 9)
+    xt.wait_recv()
+    yt.wait_recv()
+    add(out_ref, 0, half, [(part(s), 0), (rs.at[3], 0), (rx, 0), (ry, 0)])
+    yb.wait_recv()
+    xb.wait_recv()
+    add(out_ref, half, half, [(part(s), half), (rs.at[3], half), (rx, half), (ry, half)])
+    for c in (*cs, dt, db, xt, yb, yt, xb):
+        c.wait_send()
+
+
+def scatter_columns(x, cid):
+    rows, whole = x.shape
+    width = whole // lax.axis_size("seq")
+    b = x.dtype
+    return pl.pallas_call(
+        functools.partial(_scatter_kernel, rows, width),
+        out_shape=jax.ShapeDtypeStruct((rows, width), b),
+        in_specs=[pl.BlockSpec(memory_space=VMEM)],
+        out_specs=pl.BlockSpec(memory_space=VMEM),
+        scratch_shapes=[
+            VMEM((4, rows, width), b),
+            VMEM((3, rows, width), b),
+            VMEM((2, rows // 2, width), b),
+            VMEM((rows, width), b),
+            VMEM((rows, width), b),
+            pltpu.SemaphoreType.DMA((10,)),
+            pltpu.SemaphoreType.DMA((10,)),
+        ],
+        compiler_params=pltpu.CompilerParams(
+            collective_id=cid, has_side_effects=True, vmem_limit_bytes=40 << 20
+        ),
+    )(x)
+
+
+def by_heads(
+    query_proj,
+    key_proj,
+    value_proj,
+    residual,
+    out_weight,
+    expert_ids,
+    gate_values,
+    w_gate,
+    w_up,
+    w_down,
+):
+    n_seq, groups = lax.axis_size("seq"), lax.axis_size("exp")
+    block = query_proj.shape[0]
+    tokens = n_seq * block
+    tok_sub = residual.shape[0]
+    width = residual.shape[1] // n_seq
+    plane = n_seq * tok_sub
+    capacity = max(2, (3 * tok_sub * TOP + 2 * groups - 1) // (2 * groups))
+    bf, f32 = jnp.bfloat16, jnp.float32
+    meta = jnp.concatenate(
+        [expert_ids.T.astype(f32), gate_values.T, jnp.zeros((8 - 2 * TOP, tok_sub), f32)], axis=0
+    )
+    meta = jnp.pad(meta, ((0, 0), (0, 128 - tok_sub)))
+    head = ("col", HD, "row", block)
+    q, k, v, res, meta = exchange(
+        "seq",
+        (head, head, head, ("col", width, "row", tok_sub), ("all", 0, "row", 8)),
+        (query_proj, key_proj, value_proj, residual, meta),
+        [jax.ShapeDtypeStruct((tokens, HD), bf)] * 3
+        + [jax.ShapeDtypeStruct((plane, width), bf), jax.ShapeDtypeStruct((8 * n_seq, 128), f32)],
+        0,
+    )
+    qf = features(q).reshape(n_seq, block, HD)
+    kf = features(k).reshape(n_seq, block, HD)
+    vr = v.reshape(n_seq, block, HD)
+    states = jnp.einsum("btd,bte->bde", kf, vr, preferred_element_type=f32)
+    running, before_it = jnp.zeros_like(states[0]), []
+    for b in range(n_seq):
+        before_it.append(running)
+        running = running + states[b]
+    prefix = jnp.stack(before_it).astype(bf)
+    scores = jnp.einsum("btd,bsd->bts", qf, kf, preferred_element_type=f32)
+    causal = jnp.arange(block)[:, None] >= jnp.arange(block)[None, :]
+    weights = jnp.where(causal[None], scores, 0.0).astype(bf)
+    combined = jnp.einsum("bts,bse->bte", weights, vr, preferred_element_type=f32)
+    combined = combined + jnp.einsum("btd,bde->bte", qf, prefix, preferred_element_type=f32)
+    normed = combined * lax.rsqrt(jnp.mean(combined * combined, axis=-1, keepdims=True) + 1e-06)
+    normed = normed.astype(bf).reshape(n_seq, groups, tok_sub, HD)
+    normed = normed.transpose(1, 0, 2, 3).reshape(tokens, HD)
+
+    partial_out = times_rows(gather_columns(normed, 1), out_weight).astype(bf)
+    (parts,) = exchange(
+        "exp",
+        (("row", plane, "row", plane),),
+        (partial_out,),
+        [jax.ShapeDtypeStruct((tokens, width), bf)],
+        2,
+    )
+    summed = jnp.sum(parts.reshape(groups, plane, width).astype(f32), axis=0)
+    mixed_in = (res.astype(f32) + summed).astype(bf)
+
+    meta = meta.reshape(n_seq, 8, 128)
+    ids = meta[:, :TOP, :tok_sub].astype(jnp.int32).transpose(0, 2, 1)
+    gates = meta[:, TOP : 2 * TOP, :tok_sub].transpose(0, 2, 1).reshape(plane, TOP)
+    chosen = ids.reshape(n_seq, tok_sub * TOP)
+    onehot = (chosen[:, :, None] == jnp.arange(groups, dtype=jnp.int32)).astype(jnp.int32)
+    earlier = (jnp.arange(tok_sub * TOP)[:, None] > jnp.arange(tok_sub * TOP)[None, :])
+    before = jnp.sum(earlier[None, :, :, None] * onehot[:, None, :, :], axis=2)
+    slot = jnp.sum(before * onehot, axis=2)
+    target = (chosen * n_seq + jnp.arange(n_seq, dtype=jnp.int32)[:, None]) * capacity + slot
+    target = target.reshape(plane, TOP)
+    slots = jnp.arange(groups * n_seq * capacity, dtype=jnp.int32)
+    picks = [(target[:, j : j + 1] == slots[None, :]).astype(bf) for j in range(TOP)]
+    placing = picks[0]
+    for p in picks[1:]:
+        placing = placing + p
+    outgoing = lax.dot_general(
+        placing, mixed_in, (((0,), (0,)), ((), ())), preferred_element_type=f32
+    ).astype(bf)
+    load = n_seq * capacity
+    rows_shape = [jax.ShapeDtypeStruct((groups * load, width), bf)]
+    (arrived,) = exchange("exp", (("row", load, "row", load),), (outgoing,), rows_shape, 3)
+    rows = gather_columns(arrived, 4)
+    gate_act = times_rows(rows, w_gate[0])
+    up_act = times_rows(rows, w_up[0])
+    activated = (jax.nn.silu(gate_act) * up_act).astype(bf)
+    down = jnp.dot(activated, w_down[0], preferred_element_type=f32).astype(bf)
+    sums = scatter_columns(down, 5)
+    (returned,) = exchange("exp", (("row", load, "row", load),), (sums,), rows_shape, 6)
+    mixed = mixed_in.astype(f32)
+    extra = jnp.zeros_like(mixed)
+    for j in range(TOP):
+        picked = jnp.dot(picks[j], returned, preferred_element_type=f32)
+        extra = extra + gates[:, j : j + 1] * picked
+    mixed = (mixed + extra).astype(bf)
+    (out,) = exchange(
+        "seq",
+        (("row", tok_sub, "col", width),),
+        (mixed,),
+        [jax.ShapeDtypeStruct(residual.shape, bf)],
+        7,
+    )
+    return out
+
+
 def solution(mesh):
     return jax.shard_map(
-        local,
+        by_heads if mesh.shape["seq"] == 8 and mesh.shape["exp"] == 4 else local,
         mesh=mesh,
         in_specs=(
             P("seq", "exp"),

time: 335 us -> 180 us (0.54); the launches traced: 329 us -> 180 us
  waiting for transfers between devices: 224 us -> 0 us
  Pallas kernels: 0 us -> 130 us
  blocking collectives: 21.9 us -> 0 us
  between operations: 13.3 us -> 0.41 us
  other arithmetic: 13.9 us -> 2.85 us
  matrix products: 46.1 us -> 35.6 us
  local copies, waits for them, and re-layouts: 5.19 us -> 10.9 us
  starting transfers between devices: 5.06 us -> 0 us
    all_gather x3 -> x0, waiting for transfers between devices: 134 us -> none  [the longest x1 63.6 us: local(): lax.all_gather(out_weight, 'seq', axis=0, tiled=True)]
    pallas_call x0 -> x8, Pallas kernels: none -> 130 us  [the longest x5 70 us: exchange(): pl.pallas_call(functools.partial(_exchange_kernel, axis, n, kinds), out_s...]
    reduce_scatter x2 -> x0, waiting for transfers between devices: 73.1 us -> none  [the longest x1 53.6 us: local(): lax.psum_scatter(jnp.dot(rows_part, down_local, preferred_element_type=jn...]
    all_to_all x1 -> x0, blocking collectives: 21.9 us -> none  [local(): lax.all_to_all(outgoing, 'exp', split_axis=0, concat_axis=0, tiled=True)]
    all_to_all x1 -> x0, waiting for transfers between devices: 16 us -> none  [local(): lax.all_to_all(expert_out, 'exp', split_axis=0, concat_axis=0, tiled=True)]
    select_n x9 -> x0, other arithmetic: 9.92 us -> none  [the longest x8 9.92 us: hop(): return jnp.where(reached, new, before)]
    dot_general x2, matrix products: 19.8 us -> 10.2 us  [times_rows(): lax.dot_general(left, right, (((1,), (1,)), ((), ())), preferred_element_...]
    unnamed x22 -> x37, local copies, waits for them, and re-layouts: 0.21 us -> 9.57 us
  transfers between devices with their start and end apart: 6 -> 0, of which waited for: 6 -> 0; matrix products, arithmetic and copies ran while one was open for 4% -> 0% of each run, Pallas kernels for 0% -> 0%
where the time goes in v1:
time: 180 us
  Pallas kernels  130 us (72%)
  matrix products  35.6 us (20%)
  local copies, waits for them, and re-layouts  10.9 us (6%)
  other arithmetic  2.85 us (2%)
    pallas_call x5, Pallas kernels, exchange(): pl.pallas_call(functools.partial(_exchange_kernel, axis, n, kinds), out_s...  70 us
    pallas_call x2, Pallas kernels, gather_columns(): pl.pallas_call(functools.partial(_gather_kernel, rows, width), out_shape=...  35.4 us
    pallas_call x1, Pallas kernels, scatter_columns(): pl.pallas_call(functools.partial(_scatter_kernel, rows, width), out_shape...  24.4 us
    dot_general x1, matrix products, by_heads(): down = jnp.dot(activated, w_down[0], preferred_element_type=f32).astype(bf)  23.4 us
    dot_general x2, matrix products, times_rows(): lax.dot_general(left, right, (((1,), (1,)), ((), ())), preferred_element_...  10.2 us
    unnamed x37, local copies, waits for them, and re-layouts  9.57 us

profile of v1, /device:TPU:9, one launch (start us, length us, event | category | flops | bytes accessed | tf_op | source)
XLA Modules:
  0.0 179.6 jit_solution(17558589191608338556)
XLA Ops:
  0.1 0.8 convert_bitcast_fusion
  0.9 0.7 maximum_maximum_fusion
  1.8 0.9 copy-done.5
  2.7 0.9 copy-done.6
  3.6 0.9 copy-done.7
  4.5 0.9 copy-done.8
  5.4 11.4 %shard_map.100 = (bf16[512,128]{1,0:T(8,128)(2,1)S(1)}, bf16[512,128]{1,0:T(8,128)(2,1)S(1)}, bf16[512,128]{1,0:T(8,128)(2,1)S(1)}, bf16[128,768]{1,0:T(8,128)(2,1)S(1)}, f32[64,128]{1,0:T(8,128)S(1)}) custom-call(bf16[64,1024]{1,0:T(8,128)(2,1)S(1)} %copy-done.6, bf16[64,1024]{1,0:T(8,128)(2,1)S(1)} %copy-done.7, bf16[64,1024]{1,0:T(8,128)(2,1)S(1)} %copy-done.8, ...), custom_call_target="tpu_custom_call" | custom-call | tf_op jit(solution)/shard_map/pallas_call | solution.py:171
  17.1 0.6 slice_bitcast_fusion.2
  17.8 0.6 multiply_reduce_fusion
  20.2 10.7 %shard_map.101 = bf16[512,1024]{1,0:T(8,128)(2,1)S(1)} custom-call(bf16[512,128]{1,0:T(8,128)(2,1)S(1)} %bitcast.61), custom_call_target="tpu_custom_call" | custom-call | tf_op jit(solution)/shard_map/pallas_call | solution.py:241
  31.0 1.0 convolution_convert_fusion.refs_0_
  32.0 20.7 %shard_map.102 = bf16[512,768]{1,0:T(8,128)(2,1)S(1)} custom-call(bf16[512,768]{1,0:T(8,128)(2,1)S(1)} %convolution_convert_fusion.refs_0_), custom_call_target="tpu_custom_call" | custom-call | tf_op jit(solution)/shard_map/pallas_call | solution.py:171
  52.8 0.7 copy-done.9
  53.5 0.4 convolution_convert_fusion.1.refs_0_
  54.0 15.4 %shard_map.103.in_ref = bf16[384,768]{1,0:T(8,128)(2,1)S(1)} custom-call(bf16[384,768]{1,0:T(8,128)(2,1)S(1)} %convolution_convert_fusion.1.refs_0_), custom_call_target="tpu_custom_call" | custom-call | tf_op jit(solution)/shard_map/pallas_call | solution.py:171
  69.4 24.7 %shard_map.104 = bf16[384,6144]{1,0:T(8,128)(2,1)S(1)} custom-call(bf16[384,768]{1,0:T(8,128)(2,1)S(1)} %shard_map.103.in_ref), custom_call_target="tpu_custom_call" | custom-call | tf_op jit(solution)/shard_map/pallas_call | solution.py:241
  94.2 2.1 %copy-done.1 = bf16[384,6144]{1,0:T(8,128)(2,1)} copy-done((bf16[384,6144]{1,0:T(8,128)(2,1)}, bf16[384,6144]{1,0:T(8,128)(2,1)S(1)}, u32[]{:S(2)}) %copy-start.1) | copy-done | bytes 4718616
  96.3 9.2 %fusion.4 = f32[384,1152]{1,0:T(8,128)S(1)} fusion(bf16[384,6144]{1,0:T(8,128)(2,1)S(1)} %shard_map.104, bf16[1,1152,6144]{2,1,0:T(8,128)(2,1)} %param.17), kind=kOutput, calls=%fused_computation.4 | convolution fusion | flops 5435817984 | bytes 20643840 | tf_op jit(solution)/shard_map/dot_general | solution.py:33
  105.5 23.4 %fusion.6.in_ref = bf16[384,6144]{1,0:T(8,128)(2,1)} fusion(bf16[1,1152,6144]{2,1,0:T(8,128)(2,1)} %param.19, bf16[384,6144]{1,0:T(8,128)(2,1)} %copy-done.1, bf16[1,1152,6144]{2,1,0:T(8,128)(2,1)} %param.18, f32[384,1152]{1,0:T(8,128)S(1)} %fusion.4), kind=kOutput, calls=%fused_computation.6 | convolution fusion | flops 10876649472 | bytes 39518208 | tf_op jit(solution)/shard_map/dot_general | solution.py:430
  128.9 2.3 %copy-done.2 = bf16[384,6144]{1,0:T(8,128)(2,1)S(1)} copy-done((bf16[384,6144]{1,0:T(8,128)(2,1)S(1)}, bf16[384,6144]{1,0:T(8,128)(2,1)}, u32[]{:S(2)}) %copy-start.2) | copy-done | bytes 4718616
  131.3 24.4 %shard_map.105.refs_0_ = bf16[384,768]{1,0:T(8,128)(2,1)S(1)} custom-call(bf16[384,6144]{1,0:T(8,128)(2,1)S(1)} %copy-done.2), custom_call_target="tpu_custom_call" | custom-call | tf_op jit(solution)/shard_map/pallas_call | solution.py:323
  155.7 16.1 %shard_map.106 = bf16[384,768]{1,0:T(8,128)(2,1)S(1)} custom-call(bf16[384,768]{1,0:T(8,128)(2,1)S(1)} %shard_map.105.refs_0_), custom_call_target="tpu_custom_call" | custom-call | tf_op jit(solution)/shard_map/pallas_call | solution.py:171
  172.6 6.4 %shard_map.107 = bf16[16,6144]{1,0:T(8,128)(2,1)S(1)} custom-call(bf16[128,768]{1,0:T(8,128)(2,1)S(1)} %fusion.24.refs_0_), custom_call_target="tpu_custom_call" | custom-call | tf_op jit(solution)/shard_map/pallas_call | solution.py:171
  178.9 0.7 copy.53
  (66 shorter events, 3.1 us)
Async XLA Ops:
  0.0 31.0 %copy-start = (bf16[768,1024]{1,0:T(8,128)(2,1)S(1)}, bf16[768,1024]{1,0:T(8,128)(2,1)}, u32[]{:S(2)}) copy-start(bf16[768,1024]{1,0:T(8,128)(2,1)} %param.14) | copy-start | bytes 4718596
  1.8 0.9 copy-start.5
  2.7 0.9 copy-start.6
  3.6 0.9 copy-start.7
  4.5 0.9 copy-start.8
  16.8 36.0 %copy-start.3 = (bf16[128,768]{1,0:T(8,128)(2,1)}, bf16[128,768]{1,0:T(8,128)(2,1)S(1)}, u32[]{:S(2)}) copy-start(bf16[128,768]{1,0:T(8,128)(2,1)S(1)} %get-tuple-element.10) | copy-start | bytes 589828
  19.0 33.8 %copy-start.11 = (s32[128]{0:T(128)}, s32[128]{0:T(128)S(1)}, u32[]{:S(2)}) copy-start(s32[128]{0:T(128)S(1)} %get-tuple-element.15) | copy-start | bytes 1540
  19.0 33.8 %copy-start.13 = (s32[128]{0:T(128)}, s32[128]{0:T(128)S(1)}, u32[]{:S(2)}) copy-start(s32[128]{0:T(128)S(1)} %get-tuple-element.16) | copy-start | bytes 1540
  52.8 0.7 copy-start.9
  94.1 2.1 %copy-start.1 = (bf16[384,6144]{1,0:T(8,128)(2,1)}, bf16[384,6144]{1,0:T(8,128)(2,1)S(1)}, u32[]{:S(2)}) copy-start(bf16[384,6144]{1,0:T(8,128)(2,1)S(1)} %shard_map.104) | copy-start | bytes 14155780
  128.9 2.3 %copy-start.2 = (bf16[384,6144]{1,0:T(8,128)(2,1)S(1)}, bf16[384,6144]{1,0:T(8,128)(2,1)}, u32[]{:S(2)}) copy-start(bf16[384,6144]{1,0:T(8,128)(2,1)} %fusion.6.in_ref) | copy-start | bytes 14155780
  131.2 40.6 %copy-start.14 = (s32[128]{0:T(128)S(1)}, s32[128]{0:T(128)}, u32[]{:S(2)}) copy-start(s32[128]{0:T(128)} %copy-done.13) | copy-start | bytes 1540
  131.2 40.6 %copy-start.16 = (f32[128]{0:T(128)S(1)}, f32[128]{0:T(128)}, u32[]{:S(2)}) copy-start(f32[128]{0:T(128)} %get-tuple-element.22) | copy-start | bytes 1540
  131.2 41.0 %copy-start.4 = (bf16[128,768]{1,0:T(8,128)(2,1)S(1)}, bf16[128,768]{1,0:T(8,128)(2,1)}, u32[]{:S(2)}) copy-start(bf16[128,768]{1,0:T(8,128)(2,1)} %copy-done.3) | copy-start | bytes 589828
  131.2 41.0 %copy-start.10 = (f32[128,768]{1,0:T(8,128)S(1)}, f32[128,768]{1,0:T(8,128)}, u32[]{:S(2)}) copy-start(f32[128,768]{1,0:T(8,128)} %copy-done.9) | copy-start | bytes 1179652
  131.2 41.0 %copy-start.12 = (s32[128]{0:T(128)S(1)}, s32[128]{0:T(128)}, u32[]{:S(2)}) copy-start(s32[128]{0:T(128)} %copy-done.11) | copy-start | bytes 1540
  131.2 41.0 %copy-start.15 = (f32[128]{0:T(128)S(1)}, f32[128]{0:T(128)}, u32[]{:S(2)}) copy-start(f32[128]{0:T(128)} %get-tuple-element.21) | copy-start | bytes 1540

commit v2 on v1

--- a/solution.py
+++ b/solution.py
@@ -254,16 +254,7 @@
     )(x)
 
 
-def _scatter_kernel(rows, width, in_ref, out_ref, rs, st, rd, rx, ry, send, recv):
-    s = lax.axis_index("seq")
-    sx, sy, sd, flip = _around(s)
-    sib = s + flip
-    half = rows // 2
-    step = 32
-
-    def part(i):
-        return in_ref.at[:, pl.ds(pl.multiple_of(i * width, width), width)]
-
+def _pusher(send, recv):
     def push(src, dst, to, k):
         c = pltpu.make_async_remote_copy(
             src_ref=src, dst_ref=dst, send_sem=send.at[k], recv_sem=recv.at[k],
@@ -271,6 +262,140 @@
         )
         c.start()
         return c
+
+    return push
+
+
+def _up_kernel(
+    rows, width, tile, in_ref, gate_hbm, up_hbm, out_ref, all_rows, acc, held, wsem, send, recv, own
+):
+    s = lax.axis_index("seq")
+    sx, sy, sd, flip = _around(s)
+    sib = s + flip
+    half = rows // 2
+    pair = 2 * width
+    hidden = out_ref.shape[1]
+    chips = [i // 2 for i in (s, sx, sy, sd)]
+    loads = []
+    for k, chip in enumerate(chips):
+        for m, hbm in enumerate((gate_hbm, up_hbm)):
+            c = pltpu.make_async_copy(
+                hbm.at[0, :, pl.ds(pl.multiple_of(chip * pair, pair), pair)],
+                held.at[k, m],
+                wsem.at[k, m],
+            )
+            c.start()
+            loads.append(c)
+    push = _pusher(send, recv)
+
+    def at(i, part=None):
+        cols = pl.ds(pl.multiple_of(i * width, width), width)
+        if part is None:
+            return all_rows.at[:, cols]
+        return all_rows.at[pl.ds(part * half, half), cols]
+
+    def multiply(k):
+        loads[2 * k].wait()
+        loads[2 * k + 1].wait()
+        left = pl.ds(pl.multiple_of(chips[k] * pair, pair), pair)
+
+        @pl.loop(0, hidden // tile)
+        def _(j):
+            at_j = pl.ds(pl.multiple_of(j * tile, tile), tile)
+            x = all_rows[:, left]
+            g = times_rows(x, held[k, 0, at_j, :])
+            u = times_rows(x, held[k, 1, at_j, :])
+            if k:
+                g = g + acc[0, :, at_j]
+                u = u + acc[1, :, at_j]
+            if k < 3:
+                acc[0, :, at_j] = g
+                acc[1, :, at_j] = u
+            else:
+                out_ref[:, at_j] = (g / (1.0 + jnp.exp(-g)) * u).astype(out_ref.dtype)
+
+    _greet("seq", [sx, sy, sib])
+    to_x = push(in_ref, at(s), sx, 0)
+    to_y = push(in_ref, at(s), sy, 1)
+    to_s = push(in_ref, at(s), sib, 2)
+    mine = pltpu.make_async_copy(in_ref, at(s), own)
+    mine.start()
+    to_x.wait_recv()
+    fy = push(at(sx, 0), at(sx, 0), sy, 3)
+    gx = push(at(sx), at(sx), sib, 4)
+    to_y.wait_recv()
+    fx = push(at(sy, 1), at(sy, 1), sx, 5)
+    gy = push(at(sy), at(sy), sib, 6)
+    mine.wait()
+    to_s.wait_recv()
+    multiply(0)
+    gx.wait_recv()
+    multiply(1)
+    gy.wait_recv()
+    multiply(2)
+    fy.wait_recv()
+    fx.wait_recv()
+    gd = push(at(sd), at(sd), sib, 7)
+    gd.wait_recv()
+    multiply(3)
+    for c in (to_x, to_y, to_s, fy, gx, fx, gy, gd):
+        c.wait_send()
+
+
+def gathered_up(x, w_gate, w_up, cid):
+    rows, width = x.shape
+    hidden = w_gate.shape[1]
+    n = lax.axis_size("seq")
+    return pl.pallas_call(
+        functools.partial(_up_kernel, rows, width, 384),
+        out_shape=jax.ShapeDtypeStruct((rows, hidden), x.dtype),
+        in_specs=[pl.BlockSpec(memory_space=VMEM)] + [pl.BlockSpec(memory_space=pl.ANY)] * 2,
+        out_specs=pl.BlockSpec(memory_space=VMEM),
+        scratch_shapes=[
+            VMEM((rows, n * width), x.dtype),
+            VMEM((2, rows, hidden), jnp.float32),
+            VMEM((4, 2, hidden, 2 * width), x.dtype),
+            pltpu.SemaphoreType.DMA((4, 2)),
+            pltpu.SemaphoreType.DMA((8,)),
+            pltpu.SemaphoreType.DMA((8,)),
+            pltpu.SemaphoreType.DMA,
+        ],
+        compiler_params=pltpu.CompilerParams(
+            collective_id=cid, has_side_effects=True, vmem_limit_bytes=52 << 20
+        ),
+    )(x, w_gate, w_up)
+
+
+def _down_kernel(
+    rows, width, tile, in_ref, down_hbm, out_ref, held, sb, rs, st, so, rd, rx, ry, wsem, send, recv
+):
+    s = lax.axis_index("seq")
+    sx, sy, sd, flip = _around(s)
+    sib = s + flip
+    half = rows // 2
+    step = 32
+    order = [sd + flip, sx + flip, sy + flip, sd, sx, sy, s + flip, s]
+    loads = []
+    for k, i in enumerate(order):
+        c = pltpu.make_async_copy(
+            down_hbm.at[0, :, pl.ds(pl.multiple_of(i * width, width), width)],
+            held.at[k],
+            wsem.at[k],
+        )
+        c.start()
+        loads.append(c)
+    push = _pusher(send, recv)
+
+    def product(k, dst, more=None):
+        loads[k].wait()
+
+        @pl.loop(0, width // tile)
+        def _(j):
+            at_j = pl.ds(pl.multiple_of(j * tile, tile), tile)
+            r = jnp.dot(in_ref[...], held[k, :, at_j], preferred_element_type=jnp.float32)
+            if more is not None:
+                r = r + more[:, at_j].astype(jnp.float32)
+            dst[:, at_j] = r.astype(dst.dtype)
 
     def add(dst, d0, count, terms):
         @pl.loop(0, count // step)
@@ -288,56 +413,67 @@
         return ref.at[pl.ds(half, half), :]
 
     _greet("seq", [sx, sy, sib])
-    cs = [push(part(i + flip), rs.at[k], sib, k) for k, i in enumerate((sd, sx, sy, s))]
+    cs = []
+    for k in range(3):
+        product(k, sb.at[k])
+        cs.append(push(sb.at[k], rs.at[k], sib, k))
     cs[0].wait_recv()
-    add(st.at[0], 0, rows, [(part(sd), 0), (rs.at[0], 0)])
+    product(3, st.at[0], rs.at[0])
     dt = push(top(st.at[0]), rd.at[0], sx, 4)
     db = push(bottom(st.at[0]), rd.at[1], sy, 5)
     cs[1].wait_recv()
-    add(st.at[1], 0, rows, [(part(sx), 0), (rs.at[1], 0)])
+    product(4, st.at[1], rs.at[1])
     xt = push(top(st.at[1]), top(rx), sx, 6)
     cs[2].wait_recv()
-    add(st.at[2], 0, rows, [(part(sy), 0), (rs.at[2], 0)])
+    product(5, st.at[2], rs.at[2])
     yb = push(bottom(st.at[2]), bottom(ry), sy, 7)
-    cs[3].wait_recv()
+    product(6, sb.at[3])
+    cs.append(push(sb.at[3], rs.at[3], sib, 3))
     dt.wait_recv()
     add(st.at[2], 0, half, [(st.at[2], 0), (rd.at[0], 0)])
     yt = push(top(st.at[2]), top(ry), sy, 8)
     db.wait_recv()
     add(st.at[1], half, half, [(st.at[1], half), (rd.at[1], 0)])
     xb = push(bottom(st.at[1]), bottom(rx), sx, 9)
+    cs[3].wait_recv()
+    product(7, so, rs.at[3])
     xt.wait_recv()
     yt.wait_recv()
-    add(out_ref, 0, half, [(part(s), 0), (rs.at[3], 0), (rx, 0), (ry, 0)])
+    add(out_ref, 0, half, [(so, 0), (rx, 0), (ry, 0)])
     yb.wait_recv()
     xb.wait_recv()
-    add(out_ref, half, half, [(part(s), half), (rs.at[3], half), (rx, half), (ry, half)])
+    add(out_ref, half, half, [(so, half), (rx, half), (ry, half)])
     for c in (*cs, dt, db, xt, yb, yt, xb):
         c.wait_send()
 
 
-def scatter_columns(x, cid):
-    rows, whole = x.shape
-    width = whole // lax.axis_size("seq")
+def down_scattered(x, w_down, cid):
+    rows, hidden = x.shape
+    n = lax.axis_size("seq")
+    width = w_down.shape[2] // n
     b = x.dtype
     return pl.pallas_call(
-        functools.partial(_scatter_kernel, rows, width),
+        functools.partial(_down_kernel, rows, width, 256),
         out_shape=jax.ShapeDtypeStruct((rows, width), b),
-        in_specs=[pl.BlockSpec(memory_space=VMEM)],
+        in_specs=[pl.BlockSpec(memory_space=VMEM), pl.BlockSpec(memory_space=pl.ANY)],
         out_specs=pl.BlockSpec(memory_space=VMEM),
         scratch_shapes=[
+            VMEM((n, hidden, width), b),
+            VMEM((4, rows, width), b),
             VMEM((4, rows, width), b),
             VMEM((3, rows, width), b),
+            VMEM((rows, width), jnp.float32),
             VMEM((2, rows // 2, width), b),
             VMEM((rows, width), b),
             VMEM((rows, width), b),
+            pltpu.SemaphoreType.DMA((n,)),
             pltpu.SemaphoreType.DMA((10,)),
             pltpu.SemaphoreType.DMA((10,)),
         ],
         compiler_params=pltpu.CompilerParams(
-            collective_id=cid, has_side_effects=True, vmem_limit_bytes=40 << 20
+            collective_id=cid, has_side_effects=True, vmem_limit_bytes=52 << 20
         ),
-    )(x)
+    )(x, w_down)
 
 
 def by_heads(
@@ -423,12 +559,8 @@
     load = n_seq * capacity
     rows_shape = [jax.ShapeDtypeStruct((groups * load, width), bf)]
     (arrived,) = exchange("exp", (("row", load, "row", load),), (outgoing,), rows_shape, 3)
-    rows = gather_columns(arrived, 4)
-    gate_act = times_rows(rows, w_gate[0])
-    up_act = times_rows(rows, w_up[0])
-    activated = (jax.nn.silu(gate_act) * up_act).astype(bf)
-    down = jnp.dot(activated, w_down[0], preferred_element_type=f32).astype(bf)
-    sums = scatter_columns(down, 5)
+    activated = gathered_up(arrived, w_gate, w_up, 4)
+    sums = down_scattered(activated, w_down, 5)
     (returned,) = exchange("exp", (("row", load, "row", load),), (sums,), rows_shape, 6)
     mixed = mixed_in.astype(f32)
     extra = jnp.zeros_like(mixed)

time: 180 us -> 154 us (0.86)
  matrix products: 35.6 us -> 2.97 us
  Pallas kernels: 130 us -> 143 us
  local copies, waits for them, and re-layouts: 10.9 us -> 5.14 us
    pallas_call x1 -> x2, Pallas kernels: 24.4 us -> 62.2 us  [the longest x1 35 us: gathered_up(): pl.pallas_call(functools.partial(_up_kernel, rows, width, 384), out_shape...]
    pallas_call x2 -> x1, Pallas kernels: 35.4 us -> 10.7 us  [gather_columns(): pl.pallas_call(functools.partial(_gather_kernel, rows, width), out_shape=...]
    dot_general x1 -> x0, matrix products: 23.4 us -> none  [by_heads(): down = jnp.dot(activated, w_down[0], preferred_element_type=f32).astype(bf)]
    dot_general x2 -> x1, matrix products: 10.2 us -> 1.02 us  [times_rows(): lax.dot_general(left, right, (((1,), (1,)), ((), ())), preferred_element_...]
    unnamed x37 -> x13, local copies, waits for them, and re-layouts: 9.57 us -> 4.33 us
where the time goes in v2:
time: 154 us
  Pallas kernels  143 us (93%)
  local copies, waits for them, and re-layouts  5.14 us (3%)
  matrix products  2.97 us (2%)
  other arithmetic  2.85 us (2%)
    pallas_call x5, Pallas kernels, exchange(): pl.pallas_call(functools.partial(_exchange_kernel, axis, n, kinds), out_s...  69.6 us
    pallas_call x1, Pallas kernels, gathered_up(): pl.pallas_call(functools.partial(_up_kernel, rows, width, 384), out_shape...  35 us
    pallas_call x1, Pallas kernels, down_scattered(): pl.pallas_call(functools.partial(_down_kernel, rows, width, 256), out_sha...  27.2 us
    pallas_call x1, Pallas kernels, gather_columns(): pl.pallas_call(functools.partial(_gather_kernel, rows, width), out_shape=...  10.7 us
    unnamed x13, local copies, waits for them, and re-layouts  4.33 us

profile of v2, /device:TPU:9, one launch (start us, length us, event | category | flops | bytes accessed | tf_op | source)
XLA Modules:
  0.0 153.8 jit_solution(16260367588058834968)
XLA Ops:
  0.1 0.8 convert_bitcast_fusion
  0.9 0.7 maximum_maximum_fusion
  1.8 0.9 copy-done.1
  2.7 0.9 copy-done.2
  3.6 0.9 copy-done.3
  4.5 0.9 copy-done.4
  5.4 11.4 %shard_map.100 = (bf16[512,128]{1,0:T(8,128)(2,1)S(1)}, bf16[512,128]{1,0:T(8,128)(2,1)S(1)}, bf16[512,128]{1,0:T(8,128)(2,1)S(1)}, bf16[128,768]{1,0:T(8,128)(2,1)S(1)}, f32[64,128]{1,0:T(8,128)S(1)}) custom-call(bf16[64,1024]{1,0:T(8,128)(2,1)S(1)} %copy-done.2, bf16[64,1024]{1,0:T(8,128)(2,1)S(1)} %copy-done.3, bf16[64,1024]{1,0:T(8,128)(2,1)S(1)} %copy-done.4, ...), custom_call_target="tpu_custom_call" | custom-call | tf_op jit(solution)/shard_map/pallas_call | solution.py:171
  17.2 0.6 multiply_reduce_fusion
  18.2 0.2 slice_reduce_fusion.1
  18.4 0.3 fusion.4
  18.7 0.3 fusion.32
  19.2 0.3 multiply_reduce_fusion.1
  19.7 10.7 %shard_map.101 = bf16[512,1024]{1,0:T(8,128)(2,1)S(1)} custom-call(bf16[512,128]{1,0:T(8,128)(2,1)S(1)} %bitcast.42), custom_call_target="tpu_custom_call" | custom-call | tf_op jit(solution)/shard_map/pallas_call | solution.py:241
  30.4 1.0 convolution_convert_fusion.refs_0_
  31.4 20.7 %shard_map.102 = bf16[512,768]{1,0:T(8,128)(2,1)S(1)} custom-call(bf16[512,768]{1,0:T(8,128)(2,1)S(1)} %convolution_convert_fusion.refs_0_), custom_call_target="tpu_custom_call" | custom-call | tf_op jit(solution)/shard_map/pallas_call | solution.py:171
  52.2 0.4 convolution_convert_fusion.1.refs_0_
  52.6 15.4 %shard_map.103.in_ref = bf16[384,768]{1,0:T(8,128)(2,1)S(1)} custom-call(bf16[384,768]{1,0:T(8,128)(2,1)S(1)} %convolution_convert_fusion.1.refs_0_), custom_call_target="tpu_custom_call" | custom-call | tf_op jit(solution)/shard_map/pallas_call | solution.py:171
  68.1 35.0 %shard_map.104.in_ref = bf16[384,1152]{1,0:T(8,128)(2,1)S(1)} custom-call(bf16[384,768]{1,0:T(8,128)(2,1)S(1)} %shard_map.103.in_ref, bf16[1,1152,6144]{2,1,0:T(8,128)(2,1)} %gate_hbm.1, bf16[1,1152,6144]{2,1,0:T(8,128)(2,1)} %up_hbm.1), custom_call_target="tpu_custom_call" | custom-call | tf_op jit(solution)/shard_map/pallas_call | solution.py:349
  103.1 27.2 %shard_map.105.refs_0_ = bf16[384,768]{1,0:T(8,128)(2,1)S(1)} custom-call(bf16[384,1152]{1,0:T(8,128)(2,1)S(1)} %shard_map.104.in_ref, bf16[1,1152,6144]{2,1,0:T(8,128)(2,1)} %down_hbm.1), custom_call_target="tpu_custom_call" | custom-call | tf_op jit(solution)/shard_map/pallas_call | solution.py:455
  130.3 15.8 %shard_map.106 = bf16[384,768]{1,0:T(8,128)(2,1)S(1)} custom-call(bf16[384,768]{1,0:T(8,128)(2,1)S(1)} %shard_map.105.refs_0_), custom_call_target="tpu_custom_call" | custom-call | tf_op jit(solution)/shard_map/pallas_call | solution.py:171
  146.2 0.3 convolution_multiply_fusion
  146.5 0.3 fusion.2.refs_0_
  146.8 6.3 %shard_map.107 = bf16[16,6144]{1,0:T(8,128)(2,1)S(1)} custom-call(bf16[128,768]{1,0:T(8,128)(2,1)S(1)} %fusion.2.refs_0_), custom_call_target="tpu_custom_call" | custom-call | tf_op jit(solution)/shard_map/pallas_call | solution.py:171
  153.1 0.7 copy.53
  (40 shorter events, 1.3 us)
Async XLA Ops:
  0.0 30.4 %copy-start = (bf16[768,1024]{1,0:T(8,128)(2,1)S(1)}, bf16[768,1024]{1,0:T(8,128)(2,1)}, u32[]{:S(2)}) copy-start(bf16[768,1024]{1,0:T(8,128)(2,1)} %param.14) | copy-start | bytes 4718596
  1.8 0.9 copy-start.1
  2.7 0.9 copy-start.2
  3.6 0.9 copy-start.3
  4.5 0.9 copy-start.4

commit v3 on v2

--- a/solution.py
+++ b/solution.py
@@ -129,11 +129,15 @@
     return ref
 
 
-def _greet(axis, peers):
+def _here(axis, peers):
     barrier = pltpu.get_barrier_semaphore()
     for peer in peers:
         pl.semaphore_signal(barrier, inc=1, device_id={axis: peer}, device_id_type=MESH)
-    pl.semaphore_wait(barrier, len(peers))
+
+
+def _greet(axis, peers):
+    _here(axis, peers)
+    pl.semaphore_wait(pltpu.get_barrier_semaphore(), len(peers))
 
 
 def _exchange_kernel(axis, n, kinds, *refs):
@@ -166,12 +170,12 @@
         c.wait()
 
 
-def exchange(axis, kinds, ins, out_shapes, cid):
+def exchange(axis, kinds, ins, out_shapes, cid, source=VMEM):
     n, m = lax.axis_size(axis), len(ins)
     return pl.pallas_call(
         functools.partial(_exchange_kernel, axis, n, kinds),
         out_shape=out_shapes,
-        in_specs=[pl.BlockSpec(memory_space=VMEM)] * m,
+        in_specs=[pl.BlockSpec(memory_space=source)] * m,
         out_specs=[pl.BlockSpec(memory_space=VMEM)] * m,
         scratch_shapes=[
             pltpu.SemaphoreType.DMA((m, n - 1)),
@@ -179,7 +183,7 @@
             pltpu.SemaphoreType.DMA((m,)),
         ],
         compiler_params=pltpu.CompilerParams(
-            collective_id=cid, has_side_effects=True, vmem_limit_bytes=32 << 20
+            collective_id=cid, has_side_effects=True, vmem_limit_bytes=(32 if source is VMEM else 62) << 20
         ),
     )(*ins)
 
@@ -276,6 +280,7 @@
     pair = 2 * width
     hidden = out_ref.shape[1]
     chips = [i // 2 for i in (s, sx, sy, sd)]
+    _here("seq", [sx, sy, sib])
     loads = []
     for k, chip in enumerate(chips):
         for m, hbm in enumerate((gate_hbm, up_hbm)):
@@ -314,21 +319,21 @@
             else:
                 out_ref[:, at_j] = (g / (1.0 + jnp.exp(-g)) * u).astype(out_ref.dtype)
 
-    _greet("seq", [sx, sy, sib])
+    pl.semaphore_wait(pltpu.get_barrier_semaphore(), 3)
     to_x = push(in_ref, at(s), sx, 0)
     to_y = push(in_ref, at(s), sy, 1)
     to_s = push(in_ref, at(s), sib, 2)
     mine = pltpu.make_async_copy(in_ref, at(s), own)
     mine.start()
+    mine.wait()
+    to_s.wait_recv()
+    multiply(0)
     to_x.wait_recv()
     fy = push(at(sx, 0), at(sx, 0), sy, 3)
     gx = push(at(sx), at(sx), sib, 4)
     to_y.wait_recv()
     fx = push(at(sy, 1), at(sy, 1), sx, 5)
     gy = push(at(sy), at(sy), sib, 6)
-    mine.wait()
-    to_s.wait_recv()
-    multiply(0)
     gx.wait_recv()
     multiply(1)
     gy.wait_recv()
@@ -374,7 +379,8 @@
     sib = s + flip
     half = rows // 2
     step = 32
-    order = [sd + flip, sx + flip, sy + flip, sd, sx, sy, s + flip, s]
+    order = [sd + flip, sx + flip, sd, sy + flip, sx, sy, s + flip, s]
+    _here("seq", [sx, sy, sib])
     loads = []
     for k, i in enumerate(order):
         c = pltpu.make_async_copy(
@@ -412,15 +418,17 @@
     def bottom(ref):
         return ref.at[pl.ds(half, half), :]
 
-    _greet("seq", [sx, sy, sib])
-    cs = []
-    for k in range(3):
-        product(k, sb.at[k])
-        cs.append(push(sb.at[k], rs.at[k], sib, k))
+    product(0, sb.at[0])
+    pl.semaphore_wait(pltpu.get_barrier_semaphore(), 3)
+    cs = [push(sb.at[0], rs.at[0], sib, 0)]
+    product(1, sb.at[1])
+    cs.append(push(sb.at[1], rs.at[1], sib, 1))
     cs[0].wait_recv()
-    product(3, st.at[0], rs.at[0])
+    product(2, st.at[0], rs.at[0])
     dt = push(top(st.at[0]), rd.at[0], sx, 4)
     db = push(bottom(st.at[0]), rd.at[1], sy, 5)
+    product(3, sb.at[2])
+    cs.append(push(sb.at[2], rs.at[2], sib, 2))
     cs[1].wait_recv()
     product(4, st.at[1], rs.at[1])
     xt = push(top(st.at[1]), top(rx), sx, 6)
@@ -508,6 +516,7 @@
         [jax.ShapeDtypeStruct((tokens, HD), bf)] * 3
         + [jax.ShapeDtypeStruct((plane, width), bf), jax.ShapeDtypeStruct((8 * n_seq, 128), f32)],
         0,
+        pl.ANY,
     )
     qf = features(q).reshape(n_seq, block, HD)
     kf = features(k).reshape(n_seq, block, HD)

time: 154 us -> 152 us (0.987)
  local copies, waits for them, and re-layouts: 5.14 us -> 2.94 us
  Pallas kernels: 143 us -> 141 us
    unnamed x13 -> x9, local copies, waits for them, and re-layouts: 4.33 us -> 0.71 us
    pallas_call x1, Pallas kernels: 35 us -> 31.6 us  [gathered_up(): pl.pallas_call(functools.partial(_up_kernel, rows, width, 384), out_shape...]
where the time goes in v3:
time: 152 us
  Pallas kernels  141 us (93%)
  matrix products  3.88 us (3%)
  other arithmetic  3.86 us (3%)
  local copies, waits for them, and re-layouts  2.94 us (2%)
    pallas_call x5, Pallas kernels, exchange(): pl.pallas_call(functools.partial(_exchange_kernel, axis, n, kinds), out_s...  70.7 us
    pallas_call x1, Pallas kernels, gathered_up(): pl.pallas_call(functools.partial(_up_kernel, rows, width, 384), out_shape...  31.6 us
    pallas_call x1, Pallas kernels, down_scattered(): pl.pallas_call(functools.partial(_down_kernel, rows, width, 256), out_sha...  28 us
    pallas_call x1, Pallas kernels, gather_columns(): pl.pallas_call(functools.partial(_gather_kernel, rows, width), out_shape=...  10.7 us

profile of v3, /device:TPU:9, one launch (start us, length us, event | category | flops | bytes accessed | tf_op | source)
XLA Modules:
  0.0 152.0 jit_solution(273545751881017209)
XLA Ops:
  0.1 0.8 convert_bitcast_fusion
  0.9 0.7 maximum_maximum_fusion
  1.6 0.6 pad.4.refs_4_
  2.3 12.5 %shard_map.100 = (bf16[512,128]{1,0:T(8,128)(2,1)}, bf16[512,128]{1,0:T(8,128)(2,1)}, bf16[512,128]{1,0:T(8,128)(2,1)}, bf16[128,768]{1,0:T(8,128)(2,1)}, f32[64,128]{1,0:T(8,128)}) custom-call(bf16[64,1024]{1,0:T(8,128)(2,1)} %refs_0_.1, bf16[64,1024]{1,0:T(8,128)(2,1)} %refs_1_.1, bf16[64,1024]{1,0:T(8,128)(2,1)} %refs_2_.1, bf16[16,6144]{1,0:T(8,128)(2,1)} %refs_3_.1, ...), custom_call_target="tpu_custom_call" | custom-call | tf_op jit(solution)/shard_map/pallas_call | solution.py:175
  14.9 1.2 fusion.8
  16.0 0.8 slice_bitcast_fusion
  17.1 0.6 multiply_reduce_fusion
  18.1 0.2 slice_reduce_fusion.1
  18.3 1.2 fusion.4
  19.5 0.3 fusion.32
  20.0 0.3 multiply_reduce_fusion.1
  20.3 0.1 multiply_convert_fusion
  20.5 10.7 %shard_map.101 = bf16[512,1024]{1,0:T(8,128)(2,1)S(1)} custom-call(bf16[512,128]{1,0:T(8,128)(2,1)S(1)} %bitcast.42), custom_call_target="tpu_custom_call" | custom-call | tf_op jit(solution)/shard_map/pallas_call | solution.py:245
  31.2 1.0 convolution_convert_fusion.refs_0_
  32.3 20.7 %shard_map.102 = bf16[512,768]{1,0:T(8,128)(2,1)S(1)} custom-call(bf16[512,768]{1,0:T(8,128)(2,1)S(1)} %convolution_convert_fusion.refs_0_), custom_call_target="tpu_custom_call" | custom-call | tf_op jit(solution)/shard_map/pallas_call | solution.py:175
  53.1 0.4 convolution_convert_fusion.1.refs_0_
  53.5 15.4 %shard_map.103.in_ref = bf16[384,768]{1,0:T(8,128)(2,1)S(1)} custom-call(bf16[384,768]{1,0:T(8,128)(2,1)S(1)} %convolution_convert_fusion.1.refs_0_), custom_call_target="tpu_custom_call" | custom-call | tf_op jit(solution)/shard_map/pallas_call | solution.py:175
  68.9 31.6 %shard_map.104.in_ref = bf16[384,1152]{1,0:T(8,128)(2,1)S(1)} custom-call(bf16[384,768]{1,0:T(8,128)(2,1)S(1)} %shard_map.103.in_ref, bf16[1,1152,6144]{2,1,0:T(8,128)(2,1)} %gate_hbm.1, bf16[1,1152,6144]{2,1,0:T(8,128)(2,1)} %up_hbm.1), custom_call_target="tpu_custom_call" | custom-call | tf_op jit(solution)/shard_map/pallas_call | solution.py:354
  100.6 28.0 %shard_map.105.refs_0_ = bf16[384,768]{1,0:T(8,128)(2,1)S(1)} custom-call(bf16[384,1152]{1,0:T(8,128)(2,1)S(1)} %shard_map.104.in_ref, bf16[1,1152,6144]{2,1,0:T(8,128)(2,1)} %down_hbm.1), custom_call_target="tpu_custom_call" | custom-call | tf_op jit(solution)/shard_map/pallas_call | solution.py:463
  128.5 15.9 %shard_map.106 = bf16[384,768]{1,0:T(8,128)(2,1)S(1)} custom-call(bf16[384,768]{1,0:T(8,128)(2,1)S(1)} %shard_map.105.refs_0_), custom_call_target="tpu_custom_call" | custom-call | tf_op jit(solution)/shard_map/pallas_call | solution.py:175
  144.5 0.3 convolution_multiply_fusion
  144.8 0.3 fusion.2.refs_0_
  145.1 6.2 %shard_map.107 = bf16[16,6144]{1,0:T(8,128)(2,1)S(1)} custom-call(bf16[128,768]{1,0:T(8,128)(2,1)S(1)} %fusion.2.refs_0_), custom_call_target="tpu_custom_call" | custom-call | tf_op jit(solution)/shard_map/pallas_call | solution.py:175
  151.3 0.7 copy.53
  (36 shorter events, 1.0 us)
Async XLA Ops:
  0.0 31.2 %copy-start = (bf16[768,1024]{1,0:T(8,128)(2,1)S(1)}, bf16[768,1024]{1,0:T(8,128)(2,1)}, u32[]{:S(2)}) copy-start(bf16[768,1024]{1,0:T(8,128)(2,1)} %param.14) | copy-start | bytes 4718596
  14.9 4.7 %copy-start.2 = (bf16[512,128]{1,0:T(8,128)(2,1)S(1)}, bf16[512,128]{1,0:T(8,128)(2,1)}, u32[]{:S(2)}) copy-start(bf16[512,128]{1,0:T(8,128)(2,1)} %get-tuple-element.13) | copy-start | bytes 393220
  32.2 20.8 %copy-start.1 = (bf16[128,768]{1,0:T(8,128)(2,1)S(1)}, bf16[128,768]{1,0:T(8,128)(2,1)}, u32[]{:S(2)}) copy-start(bf16[128,768]{1,0:T(8,128)(2,1)} %get-tuple-element.10) | copy-start | bytes 589828

commit v4 on v3

--- a/solution.py
+++ b/solution.py
@@ -336,11 +336,11 @@
     gy = push(at(sy), at(sy), sib, 6)
     gx.wait_recv()
     multiply(1)
-    gy.wait_recv()
-    multiply(2)
     fy.wait_recv()
     fx.wait_recv()
     gd = push(at(sd), at(sd), sib, 7)
+    gy.wait_recv()
+    multiply(2)
     gd.wait_recv()
     multiply(3)
     for c in (to_x, to_y, to_s, fy, gx, fx, gy, gd):

time: 152 us -> 152 us (level)
  no operation moved by 1% of the time
where the time goes in v4:
time: 152 us
  Pallas kernels  141 us (93%)
  matrix products  3.87 us (3%)
  other arithmetic  3.86 us (3%)
  local copies, waits for them, and re-layouts  2.94 us (2%)
    pallas_call x5, Pallas kernels, exchange(): pl.pallas_call(functools.partial(_exchange_kernel, axis, n, kinds), out_s...  70.4 us
    pallas_call x1, Pallas kernels, gathered_up(): pl.pallas_call(functools.partial(_up_kernel, rows, width, 384), out_shape...  30.8 us
    pallas_call x1, Pallas kernels, down_scattered(): pl.pallas_call(functools.partial(_down_kernel, rows, width, 256), out_sha...  28.9 us
    pallas_call x1, Pallas kernels, gather_columns(): pl.pallas_call(functools.partial(_gather_kernel, rows, width), out_shape=...  10.7 us

profile of v4, /device:TPU:9, one launch (start us, length us, event | category | flops | bytes accessed | tf_op | source)
XLA Modules:
  0.0 151.7 jit_solution(11948430908810526848)
XLA Ops:
  0.1 0.8 convert_bitcast_fusion
  0.9 0.7 maximum_maximum_fusion
  1.6 0.6 pad.4.refs_4_
  2.3 12.5 %shard_map.100 = (bf16[512,128]{1,0:T(8,128)(2,1)}, bf16[512,128]{1,0:T(8,128)(2,1)}, bf16[512,128]{1,0:T(8,128)(2,1)}, bf16[128,768]{1,0:T(8,128)(2,1)}, f32[64,128]{1,0:T(8,128)}) custom-call(bf16[64,1024]{1,0:T(8,128)(2,1)} %refs_0_.1, bf16[64,1024]{1,0:T(8,128)(2,1)} %refs_1_.1, bf16[64,1024]{1,0:T(8,128)(2,1)} %refs_2_.1, bf16[16,6144]{1,0:T(8,128)(2,1)} %refs_3_.1, ...), custom_call_target="tpu_custom_call" | custom-call | tf_op jit(solution)/shard_map/pallas_call | solution.py:175
  14.9 1.2 fusion.8
  16.0 0.8 slice_bitcast_fusion
  17.1 0.6 multiply_reduce_fusion
  18.1 0.2 slice_reduce_fusion.1
  18.3 1.2 fusion.4
  19.5 0.3 fusion.32
  20.0 0.3 multiply_reduce_fusion.1
  20.3 0.1 multiply_convert_fusion
  20.5 10.7 %shard_map.101 = bf16[512,1024]{1,0:T(8,128)(2,1)S(1)} custom-call(bf16[512,128]{1,0:T(8,128)(2,1)S(1)} %bitcast.42), custom_call_target="tpu_custom_call" | custom-call | tf_op jit(solution)/shard_map/pallas_call | solution.py:245
  31.2 1.0 convolution_convert_fusion.refs_0_
  32.3 20.7 %shard_map.102 = bf16[512,768]{1,0:T(8,128)(2,1)S(1)} custom-call(bf16[512,768]{1,0:T(8,128)(2,1)S(1)} %convolution_convert_fusion.refs_0_), custom_call_target="tpu_custom_call" | custom-call | tf_op jit(solution)/shard_map/pallas_call | solution.py:175
  53.1 0.4 convolution_convert_fusion.1.refs_0_
  53.5 15.4 %shard_map.103.in_ref = bf16[384,768]{1,0:T(8,128)(2,1)S(1)} custom-call(bf16[384,768]{1,0:T(8,128)(2,1)S(1)} %convolution_convert_fusion.1.refs_0_), custom_call_target="tpu_custom_call" | custom-call | tf_op jit(solution)/shard_map/pallas_call | solution.py:175
  68.9 30.8 %shard_map.104.in_ref = bf16[384,1152]{1,0:T(8,128)(2,1)S(1)} custom-call(bf16[384,768]{1,0:T(8,128)(2,1)S(1)} %shard_map.103.in_ref, bf16[1,1152,6144]{2,1,0:T(8,128)(2,1)} %gate_hbm.1, bf16[1,1152,6144]{2,1,0:T(8,128)(2,1)} %up_hbm.1), custom_call_target="tpu_custom_call" | custom-call | tf_op jit(solution)/shard_map/pallas_call | solution.py:354
  99.7 28.9 %shard_map.105.refs_0_ = bf16[384,768]{1,0:T(8,128)(2,1)S(1)} custom-call(bf16[384,1152]{1,0:T(8,128)(2,1)S(1)} %shard_map.104.in_ref, bf16[1,1152,6144]{2,1,0:T(8,128)(2,1)} %down_hbm.1), custom_call_target="tpu_custom_call" | custom-call | tf_op jit(solution)/shard_map/pallas_call | solution.py:463
  128.6 16.3 %shard_map.106 = bf16[384,768]{1,0:T(8,128)(2,1)S(1)} custom-call(bf16[384,768]{1,0:T(8,128)(2,1)S(1)} %shard_map.105.refs_0_), custom_call_target="tpu_custom_call" | custom-call | tf_op jit(solution)/shard_map/pallas_call | solution.py:175
  144.9 0.3 convolution_multiply_fusion
  145.2 0.3 fusion.2.refs_0_
  145.5 5.5 %shard_map.107 = bf16[16,6144]{1,0:T(8,128)(2,1)S(1)} custom-call(bf16[128,768]{1,0:T(8,128)(2,1)S(1)} %fusion.2.refs_0_), custom_call_target="tpu_custom_call" | custom-call | tf_op jit(solution)/shard_map/pallas_call | solution.py:175
  151.0 0.7 copy.53
  (36 shorter events, 1.0 us)
Async XLA Ops:
  0.0 31.2 %copy-start = (bf16[768,1024]{1,0:T(8,128)(2,1)S(1)}, bf16[768,1024]{1,0:T(8,128)(2,1)}, u32[]{:S(2)}) copy-start(bf16[768,1024]{1,0:T(8,128)(2,1)} %param.14) | copy-start | bytes 4718596
  14.9 4.7 %copy-start.2 = (bf16[512,128]{1,0:T(8,128)(2,1)S(1)}, bf16[512,128]{1,0:T(8,128)(2,1)}, u32[]{:S(2)}) copy-start(bf16[512,128]{1,0:T(8,128)(2,1)} %get-tuple-element.13) | copy-start | bytes 393220
  32.2 20.8 %copy-start.1 = (bf16[128,768]{1,0:T(8,128)(2,1)S(1)}, bf16[128,768]{1,0:T(8,128)(2,1)}, u32[]{:S(2)}) copy-start(bf16[128,768]{1,0:T(8,128)(2,1)} %get-tuple-element.10) | copy-start | bytes 589828
